TPU v7x, 32 devices: a whole 2x2x4 slice. The times are simulated.
32 devices in a mesh: dp: 16 (over z, y, x), head: 2 (over core).
Axes of the slice: x: 2, y: 2, z: 4, core: 2. Of those that a mesh axis runs over, the one named last changes fastest.
Arguments:
- tokens: bfloat16 [32, 512, 768], P('dp'), may hold values from -6 to 6
- memory: bfloat16 [32, 20, 768], P('dp'), may hold values from -6 to 6
- query_weight: bfloat16 [768, 768], P(None, 'head'), may hold values from -0.21875 to 0.21875
- query_bias: bfloat16 [768], P('head'), may hold values from -3 to 3
- key_weight: bfloat16 [768, 768], P(None, 'head'), may hold values from -0.21875 to 0.21875
- value_weight: bfloat16 [768, 768], P(None, 'head'), may hold values from -0.21875 to 0.21875
- value_bias: bfloat16 [768], P('head'), may hold values from -3 to 3
- out_weight: bfloat16 [768, 768], P('head'), may hold values from -2.5 to 2.5
- out_bias: bfloat16 [768], replicated, may hold values from -3 to 3
- first_gain: bfloat16 [768], replicated, may hold values from 0.5 to 1.5
- first_shift: bfloat16 [768], replicated, may hold values from -3 to 3
- inner_weight: bfloat16 [768, 3072], P(None, 'head'), may hold values from -0.21875 to 0.21875
- inner_bias: bfloat16 [3072], P('head'), may hold values from -3 to 3
- outer_weight: bfloat16 [3072, 768], P('head'), may hold values from -0.109375 to 0.109375
- outer_bias: bfloat16 [768], replicated, may hold values from -3 to 3
- second_gain: bfloat16 [768], replicated, may hold values from 0.5 to 1.5
- second_shift: bfloat16 [768], replicated, may hold values from -3 to 3
- masked_rows: int32 [32, 80], P('dp'), may hold values from 0 to 511, as said below
- cotangent: bfloat16 [32, 80, 768], P('dp'), may hold values from -6 to 6
Outputs:
- layer_out: bfloat16 [32, 512, 768], P('dp', 'head')
- memory_out: bfloat16 [32, 20, 768], P('dp', 'head')
- tokens_grad: bfloat16 [32, 512, 768], P('dp', 'head')
- memory_grad: bfloat16 [32, 20, 768], P('dp', 'head')
- query_weight_grad: float32 [768, 768], P(None, 'head')
- query_bias_grad: float32 [768], P('head')
- key_weight_grad: float32 [768, 768], P(None, 'head')
- value_weight_grad: float32 [768, 768], P(None, 'head')
- value_bias_grad: float32 [768], P('head')
- out_weight_grad: float32 [768, 768], P('head')
- out_bias_grad: float32 [768], replicated
- first_gain_grad: float32 [768], replicated
- first_shift_grad: float32 [768], replicated
- inner_weight_grad: float32 [768, 3072], P(None, 'head')
- inner_bias_grad: float32 [3072], P('head')
- outer_weight_grad: float32 [3072, 768], P('head')
- outer_bias_grad: float32 [768], replicated
- second_gain_grad: float32 [768], replicated
- second_shift_grad: float32 [768], replicated
Inputs may be any that keep to these rules, and one draw needn't show every extreme that they name: `masked_rows`: within each segment the 80 positions are distinct token positions.
All inputs are finite; a program needn't handle non-finite values.
Results may differ from a plain program's by a relative error of at most 0.019.
Values may be sent and summed in bfloat16 or wider, within the bound.
A program may use at most 192 MiB of HBM per device.

v0:
```python
import math

import jax
import jax.numpy as jnp
from jax import lax
from jax.sharding import PartitionSpec as P

HDIM = 64


norm_eps = 1e-12
root_half = 1.0 / math.sqrt(2.0)
gauss_norm = 1.0 / math.sqrt(2.0 * math.pi)


def norm_forward(values, gain_vector, shift_vector):
    center = values - jnp.mean(values, axis=-1, keepdims=True)
    inverse = lax.rsqrt(jnp.mean(center * center, axis=-1, keepdims=True) + norm_eps)
    scaled = center * inverse
    return (scaled * gain_vector + shift_vector, scaled, inverse)


def norm_backward(upstream, scaled, inverse, gain_vector):
    weighted = upstream * gain_vector
    plain_mean = jnp.mean(weighted, axis=-1, keepdims=True)
    cross_mean = jnp.mean(weighted * scaled, axis=-1, keepdims=True)
    return inverse * (weighted - plain_mean - scaled * cross_mean)


def gelu_slope(pre_act):
    return (
        0.5 * (1.0 + lax.erf(pre_act * root_half))
        + pre_act * jnp.exp(-0.5 * pre_act * pre_act) * gauss_norm
    )


def own_rows(values):
    share = values.shape[1] // lax.axis_size("head")
    return lax.dynamic_slice_in_dim(values, lax.axis_index("head") * share, share, 1)


def own_halves(values, mem_len):
    return jnp.concatenate([own_rows(values[:, :mem_len]), own_rows(values[:, mem_len:])], axis=1)


def row_sum(values):
    return jnp.sum(values, axis=(0, 1))


def product(form, left, right):
    return jnp.einsum(form, left, right, preferred_element_type=jnp.float32)


def on_device(
    tokens,
    memory,
    query_weight,
    query_bias,
    key_weight,
    value_weight,
    value_bias,
    out_weight,
    out_bias,
    first_gain,
    first_shift,
    inner_weight,
    inner_bias,
    outer_weight,
    outer_bias,
    second_gain,
    second_shift,
    masked_rows,
    cotangent,
):
    seg_count, seq_len, feature_count = tokens.shape
    mem_len = memory.shape[1]
    all_rows = mem_len + seq_len
    local_heads = query_weight.shape[1] // HDIM
    own_mem = mem_len // lax.axis_size("head")
    score_scale = 1.0 / math.sqrt(HDIM)
    seg_index = jnp.arange(seg_count, dtype=jnp.int32)[:, None]

    def heads_view(values):
        return values.reshape(seg_count, all_rows, local_heads, HDIM)

    def flat_view(values):
        return values.reshape(seg_count, all_rows, local_heads * HDIM)

    rows_low = jnp.concatenate([memory, tokens], axis=1)
    rows_full = rows_low.astype(jnp.float32)
    query_low = (product("srd,de->sre", rows_low, query_weight) + query_bias).astype(jnp.bfloat16)
    key_low = product("srd,de->sre", rows_low, key_weight).astype(jnp.bfloat16)
    value_low = (product("srd,de->sre", rows_low, value_weight) + value_bias).astype(jnp.bfloat16)
    query_heads = heads_view(query_low)
    key_heads = heads_view(key_low)
    value_heads = heads_view(value_low)

    def head_scores():
        return product("sqhd,skhd->shqk", query_heads, key_heads) * score_scale

    scores = head_scores()
    row_peak = jnp.max(scores, axis=-1, keepdims=True)
    log_total = row_peak + jnp.log(jnp.sum(jnp.exp(scores - row_peak), axis=-1, keepdims=True))
    probs_low = jnp.exp(scores - log_total).astype(jnp.bfloat16)
    context_low = flat_view(product("shqk,skhd->sqhd", probs_low, value_heads)).astype(jnp.bfloat16)
    attention_part = product("sre,ed->srd", context_low, out_weight)
    attention_pieces = (
        lax.psum_scatter(
            attention_part[:, :mem_len].astype(jnp.bfloat16),
            "head",
            scatter_dimension=1,
            tiled=True,
        ).astype(jnp.float32),
        lax.psum_scatter(
            attention_part[:, mem_len:].astype(jnp.bfloat16),
            "head",
            scatter_dimension=1,
            tiled=True,
        ).astype(jnp.float32),
    )
    attention = jnp.concatenate(attention_pieces, axis=1) + out_bias
    normed, first_scaled, first_inverse = norm_forward(
        own_halves(rows_full, mem_len) + attention, first_gain, first_shift
    )
    normed_own_low = normed.astype(jnp.bfloat16)
    normed_pieces = (
        lax.all_gather(normed_own_low[:, :own_mem], "head", axis=1, tiled=True),
        lax.all_gather(normed_own_low[:, own_mem:], "head", axis=1, tiled=True),
    )
    normed_low = jnp.concatenate(normed_pieces, axis=1)
    inner_act = product("srd,df->srf", normed_low, inner_weight) + inner_bias
    activated = jax.nn.gelu(inner_act, approximate=False).astype(jnp.bfloat16)
    outer_part = product("srf,fd->srd", activated, outer_weight)
    outer_pieces = (
        lax.psum_scatter(
            outer_part[:, :mem_len].astype(jnp.bfloat16), "head", scatter_dimension=1, tiled=True
        ).astype(jnp.float32),
        lax.psum_scatter(
            outer_part[:, mem_len:].astype(jnp.bfloat16), "head", scatter_dimension=1, tiled=True
        ).astype(jnp.float32),
    )
    result_own, second_scaled, second_inverse = norm_forward(
        normed + jnp.concatenate(outer_pieces, axis=1) + outer_bias, second_gain, second_shift
    )
    memory_out = result_own[:, :own_mem].astype(jnp.bfloat16)
    layer_out = result_own[:, own_mem:].astype(jnp.bfloat16)
    token_upstream = (
        jnp.zeros((seg_count, seq_len, feature_count), jnp.float32)
        .at[seg_index, masked_rows]
        .add(cotangent.astype(jnp.float32))
    )
    upstream = jnp.concatenate(
        [jnp.zeros((seg_count, mem_len, feature_count), jnp.float32), token_upstream], axis=1
    )
    upstream_own = own_halves(upstream, mem_len)
    second_in_grad = norm_backward(upstream_own, second_scaled, second_inverse, second_gain)
    second_gain_part = row_sum(upstream_own * second_scaled)
    second_shift_part = row_sum(upstream_own)
    second_grad_low = second_in_grad.astype(jnp.bfloat16)
    grad_pieces = (
        lax.all_gather(second_grad_low[:, :own_mem], "head", axis=1, tiled=True),
        lax.all_gather(second_grad_low[:, own_mem:], "head", axis=1, tiled=True),
    )
    outer_grad = jnp.concatenate(grad_pieces, axis=1)
    outer_bias_part = row_sum(own_halves(outer_grad, mem_len).astype(jnp.float32))
    outer_weight_grad = product("srf,srd->fd", activated, outer_grad)
    inner_grad = (product("srd,fd->srf", outer_grad, outer_weight) * gelu_slope(inner_act)).astype(
        jnp.bfloat16
    )
    inner_weight_grad = product("srd,srf->df", normed_low, inner_grad)
    inner_bias_grad = row_sum(inner_grad.astype(jnp.float32))
    back_part = product("srf,df->srd", inner_grad, inner_weight)
    back_pieces = (
        lax.psum_scatter(
            back_part[:, :mem_len].astype(jnp.bfloat16), "head", scatter_dimension=1, tiled=True
        ).astype(jnp.float32),
        lax.psum_scatter(
            back_part[:, mem_len:].astype(jnp.bfloat16), "head", scatter_dimension=1, tiled=True
        ).astype(jnp.float32),
    )
    normed_grad = second_in_grad + jnp.concatenate(back_pieces, axis=1)
    first_in_grad = norm_backward(normed_grad, first_scaled, first_inverse, first_gain)
    first_gain_part = row_sum(normed_grad * first_scaled)
    first_shift_part = row_sum(normed_grad)
    first_grad_low = first_in_grad.astype(jnp.bfloat16)
    attention_pieces_back = (
        lax.all_gather(first_grad_low[:, :own_mem], "head", axis=1, tiled=True),
        lax.all_gather(first_grad_low[:, own_mem:], "head", axis=1, tiled=True),
    )
    attention_grad = jnp.concatenate(attention_pieces_back, axis=1)
    out_bias_part = row_sum(own_halves(attention_grad, mem_len).astype(jnp.float32))
    out_weight_grad = product("sre,srd->ed", context_low, attention_grad)
    context_grad = heads_view(
        product("srd,ed->sre", attention_grad, out_weight).astype(jnp.bfloat16)
    )
    scores_again = head_scores()
    probs = jnp.exp(scores_again - log_total)
    probs_again_low = probs.astype(jnp.bfloat16)
    probs_grad = product("sqhd,skhd->shqk", context_grad, value_heads)
    score_grad = (
        probs * (probs_grad - jnp.sum(probs * probs_grad, axis=-1, keepdims=True))
    ).astype(jnp.bfloat16)
    value_grad = flat_view(product("shqk,sqhd->skhd", probs_again_low, context_grad)).astype(
        jnp.bfloat16
    )
    query_grad = flat_view(product("shqk,skhd->sqhd", score_grad, key_heads) * score_scale).astype(
        jnp.bfloat16
    )
    key_grad = flat_view(product("shqk,sqhd->skhd", score_grad, query_heads) * score_scale).astype(
        jnp.bfloat16
    )
    query_weight_grad = product("srd,sre->de", rows_low, query_grad)
    query_bias_grad = row_sum(query_grad.astype(jnp.float32))
    key_weight_grad = product("srd,sre->de", rows_low, key_grad)
    value_weight_grad = product("srd,sre->de", rows_low, value_grad)
    value_bias_grad = row_sum(value_grad.astype(jnp.float32))
    input_part = product("sre,de->srd", query_grad, query_weight)
    input_part = input_part + product("sre,de->srd", key_grad, key_weight)
    input_part = input_part + product("sre,de->srd", value_grad, value_weight)
    input_pieces = (
        lax.psum_scatter(
            input_part[:, :mem_len].astype(jnp.bfloat16), "head", scatter_dimension=1, tiled=True
        ).astype(jnp.float32),
        lax.psum_scatter(
            input_part[:, mem_len:].astype(jnp.bfloat16), "head", scatter_dimension=1, tiled=True
        ).astype(jnp.float32),
    )
    memory_grad = (input_pieces[0] + first_in_grad[:, :own_mem]).astype(jnp.bfloat16)
    tokens_grad = (input_pieces[1] + first_in_grad[:, own_mem:]).astype(jnp.bfloat16)
    shared_grads = lax.psum(
        (
            out_bias_part,
            first_gain_part,
            first_shift_part,
            outer_bias_part,
            second_gain_part,
            second_shift_part,
        ),
        ("dp", "head"),
    )
    (
        query_weight_grad,
        query_bias_grad,
        key_weight_grad,
        value_weight_grad,
        value_bias_grad,
        out_weight_grad,
        inner_weight_grad,
        inner_bias_grad,
        outer_weight_grad,
    ) = lax.psum(
        (
            query_weight_grad,
            query_bias_grad,
            key_weight_grad,
            value_weight_grad,
            value_bias_grad,
            out_weight_grad,
            inner_weight_grad,
            inner_bias_grad,
            outer_weight_grad,
        ),
        "dp",
    )
    return (
        layer_out,
        memory_out,
        tokens_grad,
        memory_grad,
        query_weight_grad,
        query_bias_grad,
        key_weight_grad,
        value_weight_grad,
        value_bias_grad,
        out_weight_grad,
        shared_grads[0],
        shared_grads[1],
        shared_grads[2],
        inner_weight_grad,
        inner_bias_grad,
        outer_weight_grad,
        shared_grads[3],
        shared_grads[4],
        shared_grads[5],
    )


def solution(mesh):
    return jax.shard_map(
        on_device,
        mesh=mesh,
        in_specs=(
            P("dp", None, None),
            P("dp", None, None),
            P(None, "head"),
            P("head"),
            P(None, "head"),
            P(None, "head"),
            P("head"),
            P("head", None),
            P(),
            P(),
            P(),
            P(None, "head"),
            P("head"),
            P("head", None),
            P(),
            P(),
            P(),
            P("dp", None),
            P("dp", None, None),
        ),
        out_specs=(
            P("dp", "head", None),
            P("dp", "head", None),
            P("dp", "head", None),
            P("dp", "head", None),
            P(None, "head"),
            P("head"),
            P(None, "head"),
            P(None, "head"),
            P("head"),
            P("head", None),
            P(),
            P(),
            P(),
            P(None, "head"),
            P("head"),
            P("head", None),
            P(),
            P(),
            P(),
        ),
        check_vma=False,
    )
```

profile of v0, /device:TPU:0, one launch (start us, length us, event | category | flops | bytes accessed | tf_op | source)
XLA Modules:
  0.0 700.4 jit_solution(3655079491790250960)
XLA Ops:
  9.6 2.6 add_convert_fusion.3
  12.2 1.3 copy.81
  13.5 2.6 add_convert_fusion.2
  16.1 1.3 copy.82
  17.4 3.5 convolution_convert_fusion.4
  20.9 1.7 copy.83
  22.6 9.6 %multiply_reduce_fusion.1 = (f32[2,6,532]{2,1,0:T(8,128)S(1)}, f32[2,6,532,532]{2,3,1,0:T(8,128)}) fusion(bf16[2,532,6,64]{1,3,2,0:T(8,128)(2,1)} %bitcast.102, bf16[2,532,6,64]{1,3,2,0:T(8,128)(2,1)S(1)} %bitcast.98), kind=kOutput, calls=%fused_computation.5 | convolution fusion | flops 441511040 | bytes 15244992 | tf_op jit(solution)/shard_map/sqhd,skhd->shqk/dot_general | solution.py:51
  32.2 8.6 %exponential_reduce_fusion = f32[2,6,532]{2,1,0:T(8,128)S(1)} fusion(f32[2,6,532,532]{2,3,1,0:T(8,128)} %get-tuple-element.110, f32[2,6,532]{2,1,0:T(8,128)S(1)} %get-tuple-element.109), kind=kLoop, calls=%fused_computation.4 | loop fusion | flops 10182480 | bytes 13636224 | tf_op jit(solution)/shard_map/reduce_sum | solution.py:103
  40.9 8.9 %convolution_convert_fusion.2 = bf16[2,6,64,532]{3,2,1,0:T(8,128)(2,1)S(1)} fusion(bf16[2,532,6,64]{1,3,2,0:T(8,128)(2,1)S(1)} %bitcast.104, f32[2,6,532,532]{2,3,1,0:T(8,128)} %get-tuple-element.110, f32[2,6,532]{2,1,0:T(8,128)S(1)} %log_add_fusion), kind=kOutput, calls=%fused_computation.84 | convolution fusion | flops 445322304 | bytes 15244992 | tf_op jit(solution)/shard_map/shqk,skhd->sqhd/dot_general | solution.py:51
  53.0 1.5 slice.95
  54.6 1.7 fusion.59
  57.0 1.9 slice.93
  62.0 4.3 all-reduce.1
  67.3 2.7 constant_dynamic-slice_fusion.5
  70.0 2.2 fusion.62
  76.6 1.8 all_gather.18
  78.5 9.6 %all-gather.4.cloned.1.call-done = bf16[2,512,768]{2,1,0:T(8,128)(2,1)} async-done(((bf16[2,256,768]{2,1,0:T(8,128)(2,1)}), bf16[2,512,768]{2,1,0:T(8,128)(2,1)}) %all-gather.4.cloned.1.call-update) | async-done | bytes 1572880 | tf_op jit(solution)/shard_map/all_gather | solution.py:128
  88.1 5.9 fusion.30
  94.0 15.4 %fusion.3 = bf16[2,532,1536]{2,1,0:T(8,128)(2,1)S(1)} fusion(f32[2,532,1536]{2,1,0:T(8,128)S(1)} %get-tuple-element.111, f32[1536]{0:T(1024)S(1)} %convert_element_type.170, u8[532,1536]{1,0:T(8,128)(4,1)S(1)} %get-tuple-element.77, u8[532,1536]{1,0:T(8,128)(4,1)S(1)} %get-tuple-element.76), kind=kLoop, calls=%fused_computation.11 | loop fusion | flops 116035584 | bytes 11446272 | tf_op jit(solution)/shard_map/convert_element_type | solution.py:132
  109.5 2.8 fusion.26
  112.3 1.2 copy-done.20
  113.5 1.7 slice.99
  115.3 1.8 bitcast_convert_fusion
  117.1 1.9 broadcast_in_dim.6
  118.9 22.7 %scatter_fusion = f32[2,512,768]{2,1,0:T(8,128)} fusion(f32[2,512,768]{2,1,0:T(8,128)} %broadcast_in_dim.6, s32[160]{0:T(256)S(1)} %reshape.125, f32[160,768]{1,0:T(8,128)} %bitcast_convert_fusion), kind=kCustom, calls=%fused_computation | custom fusion | flops 122880 | bytes 1475840 | tf_op jit(solution)/shard_map/scatter-add | solution.py:150
  141.6 2.7 constant_dynamic-slice_fusion.4
  144.4 3.8 all-reduce.2
  148.3 2.6 fusion.61
  151.3 1.4 multiply_reduce_fusion.2
  156.2 1.8 all_gather.20
  158.1 8.5 %all-gather.6.cloned.1.call-done = bf16[2,512,768]{2,1,0:T(8,128)(2,1)} async-done(((bf16[2,256,768]{2,1,0:T(8,128)(2,1)}), bf16[2,512,768]{2,1,0:T(8,128)(2,1)}) %all-gather.6.cloned.1.call-update) | async-done | bytes 1572880 | tf_op jit(solution)/shard_map/all_gather | solution.py:162
  166.6 8.3 %convert_reduce_fusion = (f32[1536]{0:T(1024)}, bf16[2,532,1536]{2,1,0:T(8,128)(2,1)S(1)}) fusion(f32[2,532,1536]{2,1,0:T(8,128)} %copy-done.10, f32[1536]{0:T(1024)S(1)} %copy-done.41, bf16[1536,768]{1,0:T(8,128)(2,1)} %param.32, bf16[2,512,768]{2,1,0:T(8,128)(2,1)} %all-gather.6.cloned.1.call-done, bf16[2,20,768]{2,1,0:T(8,128)(2,1)S(1)} %copy.93), kind=kOutput, calls=%fused_computation.23 | convolution fusion | flops 2534803968 | bytes 13811712 | tf_op jit(solution)/shard_map/srd,fd->srf/dot_general | solution.py:51
  174.8 2.8 fusion.23
  177.7 1.2 copy-done.22
  178.9 1.5 slice.105
  181.4 3.6 all-reduce.3
  185.1 5.7 reduce-scatter.9.cloned.1.call-done
  190.8 4.1 multiply_reduce_fusion.3
  194.9 1.8 fusion.60
  199.5 2.1 all_gather.22
  201.6 8.2 %all-gather.8.cloned.1.call-done = bf16[2,512,768]{2,1,0:T(8,128)(2,1)} async-done(((bf16[2,256,768]{2,1,0:T(8,128)(2,1)}), bf16[2,512,768]{2,1,0:T(8,128)(2,1)}) %all-gather.8.cloned.1.call-update) | async-done | bytes 1572880 | tf_op jit(solution)/shard_map/all_gather | solution.py:188
  209.8 2.5 convolution_convert_fusion.3
  212.9 8.9 %convert_reduce_fusion.1 = (f32[6,64]{1,0:T(8,128)S(1)}, bf16[2,6,64,532]{3,2,1,0:T(8,128)(2,1)S(1)}) fusion(bf16[2,532,6,64]{1,3,2,0:T(8,128)(2,1)S(1)} %bitcast.108, f32[2,6,532,532]{2,3,1,0:T(8,128)} %get-tuple-element.110, f32[2,6,532]{2,1,0:T(8,128)S(1)} %log_add_fusion), kind=kOutput, calls=%fused_computation.47 | convolution fusion | flops 446139072 | bytes 15246528 | tf_op jit(solution)/shard_map/shqk,sqhd->skhd/dot_general | solution.py:51
  221.8 11.3 %multiply_reduce_fusion = (f32[2,6,532]{2,1,0:T(8,128)S(1)}, f32[2,6,532,532]{2,3,1,0:T(8,128)}) fusion(f32[2,6,532,532]{2,3,1,0:T(8,128)} %get-tuple-element.110, f32[2,6,532]{2,1,0:T(8,128)S(1)} %log_add_fusion, bf16[2,532,6,64]{1,3,2,0:T(8,128)(2,1)S(1)} %bitcast.109, bf16[2,532,6,64]{1,3,2,0:T(8,128)(2,1)S(1)} %bitcast.105), kind=kOutput, calls=%fused_computation.2 | convolution fusion | flops 448303616 | bytes 28855680 | tf_op jit(solution)/shard_map/sqhd,skhd->shqk/dot_general | solution.py:51
  233.1 11.9 %multiply_convert_fusion = bf16[2,6,532,532]{2,3,1,0:T(8,128)(2,1)S(1)} fusion(f32[2,6,532,532]{2,3,1,0:T(8,128)} %get-tuple-element.113, f32[2,6,532,532]{2,3,1,0:T(8,128)} %get-tuple-element.110, f32[2,6,532]{2,1,0:T(8,128)S(1)} %get-tuple-element.112, f32[2,6,532]{2,1,0:T(8,128)S(1)} %log_add_fusion), kind=kLoop, calls=%fused_computation.1 | loop fusion | flops 16981440 | bytes 34013952 | tf_op jit(solution)/shard_map/convert_element_type | solution.py:202
  245.0 2.7 multiply_convert_fusion.1
  247.7 1.8 convert_reduce_fusion.2
  254.1 1.6 slice.108
  255.8 8.0 %convolution_bitcast_fusion = f32[1536,768]{1,0:T(8,128)} fusion(bf16[2,532,1536]{2,1,0:T(8,128)(2,1)} %copy-done.19, bf16[2,512,768]{2,1,0:T(8,128)(2,1)} %all-gather.6.cloned.1.call-done, bf16[2,20,768]{2,1,0:T(8,128)(2,1)S(1)} %copy.93), kind=kOutput, calls=%fused_computation.37 | convolution fusion | flops 2513559552 | bytes 9621504 | tf_op jit(solution)/shard_map/srf,srd->fd/dot_general | solution.py:51
  263.8 5.2 convolution_bitcast_fusion.1
  269.0 2.0 convolution_bitcast_fusion.2
  271.1 2.3 convolution_bitcast_fusion.3
  273.3 2.3 convolution_bitcast_fusion.5
  275.6 2.3 convolution_bitcast_fusion.4
  278.0 1.3 constant_dynamic-slice_fusion
  281.5 3.6 all-reduce.4
  285.9 1.2 constant_dynamic-slice_fusion.2
  287.4 45.5 %all-reduce.5 = (f32[768]{0:T(1024)}, f32[768]{0:T(1024)}, f32[768]{0:T(1024)}, f32[768]{0:T(1024)}, f32[768]{0:T(1024)}, /*index=5*/f32[768]{0:T(1024)}) all-reduce(f32[768]{0:T(1024)S(1)} %convert_reduce_fusion.4, f32[768]{0:T(1024)S(1)} %get-tuple-element.78, ...), channel_id=1, replica_groups=mesh['dp'=16,'head'=2] {'dp','head'}, use_global_device_ids=true, to_apply=%region_29.0 | all-reduce | flops 4608 | bytes 36864 | tf_op jit(solution)/shard_map/psum | solution.py:230
  332.9 79.7 %all-reduce.6 = (f32[384]{0:T(512)}, f32[384]{0:T(512)}, f32[1536]{0:T(1024)}) all-reduce(f32[384]{0:T(512)S(1)} %reduce_sum.186, f32[384]{0:T(512)S(1)} %reduce_sum.188, f32[1536]{0:T(1024)S(1)} %copy-done.47), channel_id=1, replica_groups=mesh['dp'=16,'head'=2] {'dp'}, use_global_device_ids=true, to_apply=%region_22.0 | all-reduce | flops 2304 | bytes 18432 | tf_op jit(solution)/shard_map/psum | solution.py:251
  412.6 2.3 fusion.31
  414.9 266.2 %all-reduce.10.cloned.1.call-done = (f32[768,384]{1,0:T(8,128)}, f32[768,384]{1,0:T(8,128)}, f32[768,384]{1,0:T(8,128)}, f32[384,768]{1,0:T(8,128)}, f32[768,1536]{1,0:T(8,128)}, /*index=5*/f32[1536,768]{1,0:T(8,128)}) async-done(((f32[768,384]{1,0:T(8,128)}, f32[768,384]{1,0:T(8,128)}, f32[768,384]{1,0:T(8,128)}, f32[384,768]{1,0:T(8,128)}, f32[768,1536]{1,0:T(8,128)}, /*index=5*/f32[1536,768]{1,0:T(8,128)}), ...) | async-done | bytes 14155792 | tf_op jit(solution)/shard_map/psum | solution.py:251
  681.1 2.5 copy.135
  687.2 2.2 copy.139
  689.7 2.4 copy.140
  (224 shorter events, 35.4 us)
Async XLA Ops:
  7.2 80.9 %copy-start = (bf16[768,1536]{1,0:T(8,128)(2,1)S(1)}, bf16[768,1536]{1,0:T(8,128)(2,1)}, u32[]{:S(2)}) copy-start(bf16[768,1536]{1,0:T(8,128)(2,1)} %param.30) | copy-start | bytes 7077892
  7.2 62.8 %reduce-scatter.5.cloned.1.call-start = ((), (), s32[]{:S(2)}) async-start(), calls=%async_computation.4 | async-start | bytes 2359296 | tf_op jit(solution)/shard_map/reduce_scatter | solution.py:114
  9.6 45.0 %copy-start.33 = (bf16[2,20,768]{2,1,0:T(8,128)(2,1)}, bf16[2,20,768]{2,1,0:T(8,128)(2,1)S(1)}, u32[]{:S(2)}) copy-start(bf16[2,20,768]{2,1,0:T(8,128)(2,1)S(1)} %copy.80) | copy-start | bytes 184324
  32.2 8.6 %copy-start.7 = (bf16[2,532,384]{1,2,0:T(8,128)(2,1)S(1)}, bf16[2,532,384]{1,2,0:T(8,128)(2,1)}, u32[]{:S(2)}) copy-start(bf16[2,532,384]{1,2,0:T(8,128)(2,1)} %copy.81) | copy-start | bytes 2451460
  40.9 9.9 %copy-start.58 = (bf16[384,768]{1,0:T(8,128)(2,1)S(1)}, bf16[384,768]{1,0:T(8,128)(2,1)}, u32[]{:S(2)}) copy-start(bf16[384,768]{1,0:T(8,128)(2,1)} %param.26) | copy-start | bytes 1769476
  54.5 33.5 %all-gather.4.cloned.1.call-start = ((), (), s32[]{:S(2)}) async-start(), calls=%async_computation.5 | async-start | bytes 2359296 | tf_op jit(solution)/shard_map/all_gather | solution.py:128
  57.0 1.9 copy-start.49
  57.0 2.5 copy-start.50
  57.0 3.1 copy-start.51
  57.0 3.7 slice-start.4
  57.0 3.8 copy-start.60
  60.8 9.2 %copy-start.44 = (f32[768]{0:T(1024)S(1)}, f32[768]{0:T(1024)}, u32[]{:S(2)}) copy-start(f32[768]{0:T(1024)} %convert_element_type.166) | copy-start | bytes 9220
  70.0 3.4 copy-start.35
  70.0 3.4 copy-start.39
  73.4 2.4 copy-start.48
  75.7 72.6 %reduce-scatter.7.cloned.1.call-start = ((), (), s32[]{:S(2)}) async-start(), calls=%async_computation.6 | async-start | bytes 2359296 | tf_op jit(solution)/shard_map/reduce_scatter | solution.py:138
  75.8 18.2 %copy-start.40 = (f32[1536]{0:T(1024)}, f32[1536]{0:T(1024)S(1)}, u32[]{:S(2)}) copy-start(f32[1536]{0:T(1024)S(1)} %convert_element_type.170) | copy-start | bytes 18436
  78.5 15.5 %copy-start.37 = (bf16[2,20,768]{2,1,0:T(8,128)(2,1)}, bf16[2,20,768]{2,1,0:T(8,128)(2,1)S(1)}, u32[]{:S(2)}) copy-start(bf16[2,20,768]{2,1,0:T(8,128)(2,1)S(1)} %copy.89) | copy-start | bytes 184324
  94.0 15.5 %copy-start.10 = (f32[2,532,1536]{2,1,0:T(8,128)}, f32[2,532,1536]{2,1,0:T(8,128)S(1)}, u32[]{:S(2)}) copy-start(f32[2,532,1536]{2,1,0:T(8,128)S(1)} %get-tuple-element.111) | copy-start | bytes 19611652
  94.0 15.5 %copy-start.56 = (bf16[1536,768]{1,0:T(8,128)(2,1)S(1)}, bf16[1536,768]{1,0:T(8,128)(2,1)}, u32[]{:S(2)}) copy-start(bf16[1536,768]{1,0:T(8,128)(2,1)} %param.32) | copy-start | bytes 7077892
  109.5 2.8 copy-start.19
  113.4 1.7 copy-start.55
  113.5 1.8 copy-start.52
  113.5 1.8 copy-start.53
  115.1 51.4 %all-gather.6.cloned.1.call-start = ((), (), s32[]{:S(2)}) async-start(), calls=%async_computation.7 | async-start | bytes 2359296 | tf_op jit(solution)/shard_map/all_gather | solution.py:162
  141.6 2.7 slice-start.3
  148.3 3.0 copy-start.5
  150.9 1.8 copy-start.4
  152.7 2.6 copy-start.42
  154.2 12.3 %copy-start.41 = (f32[1536]{0:T(1024)S(1)}, f32[1536]{0:T(1024)}, u32[]{:S(2)}) copy-start(f32[1536]{0:T(1024)} %copy-done.40) | copy-start | bytes 18436
  155.3 35.5 %reduce-scatter.9.cloned.1.call-start = ((), (), s32[]{:S(2)}) async-start(), calls=%async_computation.8 | async-start | bytes 2359296 | tf_op jit(solution)/shard_map/reduce_scatter | solution.py:177
  174.8 2.8 copy-start.61
  178.8 11.9 %copy-start.3 = (f32[2,266,768]{2,1,0:T(8,128)S(1)}, f32[2,266,768]{2,1,0:T(8,128)}, u32[]{:S(2)}) copy-start(f32[2,266,768]{2,1,0:T(8,128)} %copy-done.2) | copy-start | bytes 4902916
  178.8 11.9 %copy-start.36 = (f32[768]{0:T(1024)S(1)}, f32[768]{0:T(1024)}, u32[]{:S(2)}) copy-start(f32[768]{0:T(1024)} %convert_element_type.167) | copy-start | bytes 9220
  178.9 12.0 %copy-start.43 = (f32[2,266]{1,0:T(2,128)S(1)}, f32[2,266]{1,0:T(2,128)}, u32[]{:S(2)}) copy-start(f32[2,266]{1,0:T(2,128)} %copy-done.42) | copy-start | bytes 6388
  180.4 29.4 %all-gather.8.cloned.1.call-start = ((), (), s32[]{:S(2)}) async-start(), calls=%async_computation.9 | async-start | bytes 2359296 | tf_op jit(solution)/shard_map/all_gather | solution.py:188
  196.6 13.2 %copy-start.59 = (bf16[384,768]{1,0:T(8,128)(2,1)S(1)}, bf16[384,768]{1,0:T(8,128)(2,1)}, u32[]{:S(2)}) copy-start(bf16[384,768]{1,0:T(8,128)(2,1)} %param.26) | copy-start | bytes 1769476
  198.6 213.9 %reduce-scatter.11.cloned.1.call-start = ((), (), s32[]{:S(2)}) async-start(), calls=%async_computation.10 | async-start | bytes 2359296 | tf_op jit(solution)/shard_map/reduce_scatter | solution.py:224
  212.9 8.9 %copy-start.8 = (bf16[2,532,384]{1,2,0:T(8,128)(2,1)S(1)}, bf16[2,532,384]{1,2,0:T(8,128)(2,1)}, u32[]{:S(2)}) copy-start(bf16[2,532,384]{1,2,0:T(8,128)(2,1)} %copy.81) | copy-start | bytes 2451460
  221.8 30.0 %copy-start.13 = (bf16[2,6,64,532]{3,2,1,0:T(8,128)(2,1)}, bf16[2,6,64,532]{3,2,1,0:T(8,128)(2,1)S(1)}, u32[]{:S(2)}) copy-start(bf16[2,6,64,532]{3,2,1,0:T(8,128)(2,1)S(1)} %get-tuple-element.117) | copy-start | bytes 2451460
  233.1 11.9 %copy-start.6 = (bf16[2,532,384]{1,2,0:T(8,128)(2,1)S(1)}, bf16[2,532,384]{1,2,0:T(8,128)(2,1)}, u32[]{:S(2)}) copy-start(bf16[2,532,384]{1,2,0:T(8,128)(2,1)} %copy.82) | copy-start | bytes 2451460
  247.7 1.8 copy-start.30
  255.7 8.1 %copy-start.38 = (bf16[2,20,768]{2,1,0:T(8,128)(2,1)S(1)}, bf16[2,20,768]{2,1,0:T(8,128)(2,1)}, u32[]{:S(2)}) copy-start(bf16[2,20,768]{2,1,0:T(8,128)(2,1)} %copy-done.37) | copy-start | bytes 184324
  255.7 425.4 %all-reduce.10.cloned.1.call-start = ((), (), s32[]{:S(2)}) async-start(), calls=%async_computation.11 | async-start | bytes 28311552 | tf_op jit(solution)/shard_map/psum | solution.py:251
  255.7 8.1 %copy-start.57 = (bf16[2,512,768]{2,1,0:T(8,128)(2,1)S(1)}, bf16[2,512,768]{2,1,0:T(8,128)(2,1)}, u32[]{:S(2)}) copy-start(bf16[2,512,768]{2,1,0:T(8,128)(2,1)} %all-gather.4.cloned.1.call-done) | copy-start | bytes 4718596
  255.7 8.0 %copy-start.62 = (bf16[2,532,1536]{2,1,0:T(8,128)(2,1)S(1)}, bf16[2,532,1536]{2,1,0:T(8,128)(2,1)}, u32[]{:S(2)}) copy-start(bf16[2,532,1536]{2,1,0:T(8,128)(2,1)} %copy-done.61) | copy-start | bytes 9805828
  263.8 5.2 copy-start.28
  263.8 5.2 copy-start.32
  269.0 2.0 copy-start.14
  269.0 2.0 copy-start.23
  269.0 2.0 copy-start.34
  277.9 1.7 copy-start.15
  277.9 3.6 slice-start
  277.9 7.3 %copy-start.9 = (f32[2,266,768]{2,1,0:T(8,128)S(1)}, f32[2,266,768]{2,1,0:T(8,128)}, u32[]{:S(2)}) copy-start(f32[2,266,768]{2,1,0:T(8,128)} %get-tuple-element.102) | copy-start | bytes 4902916
  279.6 7.8 %copy-start.45 = (f32[768]{0:T(1024)S(1)}, f32[768]{0:T(1024)}, u32[]{:S(2)}) copy-start(f32[768]{0:T(1024)} %get-tuple-element.80) | copy-start | bytes 9220
  279.6 7.8 %copy-start.46 = (f32[768]{0:T(1024)S(1)}, f32[768]{0:T(1024)}, u32[]{:S(2)}) copy-start(f32[768]{0:T(1024)} %get-tuple-element.85) | copy-start | bytes 9220
  279.6 53.3 %copy-start.47 = (f32[1536]{0:T(1024)S(1)}, f32[1536]{0:T(1024)}, u32[]{:S(2)}) copy-start(f32[1536]{0:T(1024)} %get-tuple-element.118) | copy-start | bytes 18436
  681.1 2.5 copy-start.26
  681.1 3.5 copy-start.25
  681.1 4.5 copy-start.24
  683.6 3.6 copy-start.12
  685.6 3.8 slice-start.1
  687.2 2.5 slice-start.2
  689.7 3.4 copy-start.1
  (12 other events, 13.4 us)
Sparse Core Ops, SparseCore 0:
  54.7 11.7 reduce-scatter.4
  75.8 12.2 all-gather.3
  115.3 10.2 reduce-scatter.6
  155.4 11.0 all-gather.5
  180.5 10.2 reduce-scatter.8
  198.7 11.0 all-gather.7
  255.8 10.2 reduce-scatter.10
  278.0 403.0 all-reduce.9
where the time goes:
time: 706 us; the launch traced here: 700 us
  waiting for transfers between devices  298 us (42%)
  blocking collectives  146 us (21%)
  matrix products  100 us (14%)
  other arithmetic  81.9 us (12%)
  local copies, waits for them, and re-layouts  56.9 us (8%)
  between operations  16.3 us (2%)
    psum x1, waiting for transfers between devices, on_device(): lax.psum((query_weight_grad, query_bias_grad, key_weight_grad, value_weig...  266 us
    dot_general x24, matrix products, product(): return jnp.einsum(form, left, right, preferred_element_type=jnp.float32)  100 us
    psum x1, blocking collectives, on_device(): lax.psum((query_weight_grad, query_bias_grad, key_weight_grad, value_weig...  79.7 us
    psum x1, blocking collectives, on_device(): lax.psum((out_bias_part, first_gain_part, first_shift_part, outer_bias_pa...  45.5 us
    unnamed x144, local copies, waits for them, and re-layouts  24.1 us
    scatter-add x1, other arithmetic, on_device(): token_upstream = jnp.zeros((seg_count, seq_len, feature_count), jnp.float...  22.7 us
    convert_element_type x1, other arithmetic, on_device(): activated = jax.nn.gelu(inner_act, approximate=False).astype(jnp.bfloat16)  15.4 us
    unnamed x4, blocking collectives  15.3 us
  transfers between devices with their start and end apart: 8, of which 5 were waited for; matrix products, arithmetic and copies ran while one was open for 10% of the time, Pallas kernels for 0%

commit v1 on v0

v1 whole, which is shorter than its diff:
```python
import functools
import math

import jax
import jax.numpy as jnp
from jax import lax
from jax.experimental import pallas as pl
from jax.experimental.pallas import tpu as pltpu
from jax.sharding import PartitionSpec as P

HDIM = 64
GROUP = 16
MESH = pl.DeviceIdType.MESH

norm_eps = 1e-12
root_half = 1.0 / math.sqrt(2.0)
gauss_norm = 1.0 / math.sqrt(2.0 * math.pi)
low_type = jnp.bfloat16
full_type = jnp.float32


def norm_stats(values):
    center = values - jnp.mean(values, axis=-1, keepdims=True)
    inverse = lax.rsqrt(jnp.mean(center * center, axis=-1, keepdims=True) + norm_eps)
    return center * inverse, inverse


def norm_backward(upstream, scaled, inverse, gain_vector):
    weighted = upstream * gain_vector
    plain_mean = jnp.mean(weighted, axis=-1, keepdims=True)
    cross_mean = jnp.mean(weighted * scaled, axis=-1, keepdims=True)
    return inverse * (weighted - plain_mean - scaled * cross_mean)


def gelu_slope(pre_act):
    return (
        0.5 * (1.0 + lax.erf(pre_act * root_half))
        + pre_act * jnp.exp(-0.5 * pre_act * pre_act) * gauss_norm
    )


def product(form, left, right):
    return jnp.einsum(form, left, right, preferred_element_type=jnp.float32)


def row_sum(values):
    return jnp.sum(values, axis=(0, 1))


class Place:
    def __init__(self):
        index = lax.axis_index("dp")
        self.head = lax.axis_index("head")
        base = index // GROUP * GROUP
        inner = lax.rem(index, GROUP)
        self.x = lax.rem(inner, 2)
        self.y = lax.rem(inner // 2, 2)
        self.z = inner // 4
        self.base = base
        self.twin = (index, 1 - self.head)

    def at(self, x, y, z):
        return (self.base + z * 4 + y * 2 + x, self.head)

    def axes(self, flip):
        x_next = self.at(1 - self.x, self.y, self.z)
        y_next = self.at(self.x, 1 - self.y, self.z)
        if flip:
            return self.y, self.x, y_next, x_next
        return self.x, self.y, x_next, y_next

    def z_plus(self, step):
        return lax.rem(self.z + step, 4)

    def along_z(self, step):
        return self.at(self.x, self.y, self.z_plus(step))

    def partners(self):
        found = [self.twin, self.at(1 - self.x, self.y, self.z), self.at(self.x, 1 - self.y, self.z)]
        return found + [self.along_z(step) for step in (1, 2, 3)]


def meet(place):
    barrier = pltpu.get_barrier_semaphore()
    partners = place.partners()
    for partner in partners:
        pl.semaphore_signal(barrier, inc=1, device_id=partner, device_id_type=MESH)
    pl.semaphore_wait(barrier, len(partners))


def remote(src, dst, send, recv, device):
    return pltpu.make_async_remote_copy(
        src_ref=src, dst_ref=dst, send_sem=send, recv_sem=recv, device_id=device, device_id_type=MESH
    )


class Gather:
    def __init__(self, place, all_ref, half, send, recv, twin_send, twin_recv):
        self.place, self.all, self.half = place, all_ref, half
        self.send, self.recv, self.twin_send, self.twin_recv = send, recv, twin_send, twin_recv
        self.p, self.q, self.p_next, self.q_next = place.axes(half == 1)
        self.sends = []
        self.count = 0

    def block(self, q, p, z):
        return (q * 2 + p) * 4 + z

    def ref(self, block, kind):
        return self.all.at[kind, self.half, block]

    def pass_on(self, block, device):
        ref = self.ref(block, self.place.head)
        copy = remote(ref, ref, self.send.at[self.half, self.count], self.recv.at[self.half, block], device)
        copy.start()
        self.count += 1
        self.sends.append(copy)

    def to_twin(self, block):
        ref = self.ref(block, self.place.head)
        copy = remote(
            ref, ref, self.twin_send.at[self.half, block], self.twin_recv.at[self.half, block], self.place.twin
        )
        copy.start()

    def landed(self, block):
        ref = self.ref(block, self.place.head)
        remote(
            ref, ref, self.send.at[self.half, 0], self.recv.at[self.half, block], self.p_next
        ).wait_recv()

    def start(self):
        own = self.block(self.q, self.p, self.place.z)
        for step in (1, 3, 2):
            self.pass_on(own, self.place.along_z(step))
        self.pass_on(own, self.p_next)
        self.pass_on(own, self.q_next)
        self.to_twin(own)

    def z_step(self, step):
        block = self.block(self.q, self.p, self.place.z_plus(step))
        self.landed(block)
        self.pass_on(block, self.p_next)
        self.pass_on(block, self.q_next)
        self.to_twin(block)

    def p_step(self, step):
        block = self.block(self.q, 1 - self.p, self.place.z_plus(step))
        self.landed(block)
        self.pass_on(block, self.q_next)
        self.to_twin(block)

    def q_step(self, side, step):
        p = self.p if side == 0 else 1 - self.p
        block = self.block(1 - self.q, p, self.place.z_plus(step))
        self.landed(block)
        self.to_twin(block)

    def twin_landed(self, block):
        ref = self.ref(block, 1 - self.place.head)
        remote(
            ref, ref, self.twin_send.at[self.half, 0], self.twin_recv.at[self.half, block], self.place.twin
        ).wait_recv()

    def finish(self):
        for copy in self.sends:
            copy.wait_send()
        for block in range(GROUP):
            ref = self.ref(block, self.place.head)
            remote(
                ref, ref, self.twin_send.at[self.half, block], self.twin_recv.at[self.half, block], self.place.twin
            ).wait_send()


Z_ORDER = (0, 1, 3, 2)


class Reduce:
    def __init__(self, place, slot, src_ref, out_ref, first, second, third, acc, send, recv):
        self.place, self.slot = place, slot
        self.src, self.out = src_ref, out_ref
        self.first, self.second, self.third, self.acc = first, second, third, acc
        self.send, self.recv = send, recv
        self.p, self.q, self.p_next, self.q_next = place.axes(slot % 2 == 1)
        rows = src_ref.shape[0]
        self.p_rows, self.q_rows, self.z_rows = rows // 2, rows // 4, rows // 16
        self.count = 0
        self.copies = []

    def put(self, src, dst, device):
        copy = remote(src, dst, self.send.at[self.slot, self.count], self.recv.at[self.slot, self.count], device)
        copy.start()
        self.count += 1
        self.copies.append(copy)

    def landed(self, count):
        for copy in self.copies[-count:]:
            copy.wait_recv()

    def step_1(self):
        away = (1 - self.p) * self.p_rows
        self.put(self.src.at[pl.ds(away, self.p_rows)], self.first, self.p_next)

    def step_2(self):
        self.landed(1)
        kept = self.src[pl.ds(self.p * self.p_rows, self.p_rows)].astype(full_type)
        self.acc[...] = (kept + self.first[...].astype(full_type)).astype(low_type)
        away = (1 - self.q) * self.q_rows
        self.put(self.acc.at[pl.ds(away, self.q_rows)], self.second, self.q_next)

    def step_3(self):
        self.landed(1)
        mine = pl.ds(self.q * self.q_rows, self.q_rows)
        kept = self.acc[mine].astype(full_type)
        self.acc[mine] = (kept + self.second[...].astype(full_type)).astype(low_type)
        for step in (1, 3, 2):
            away = self.q * self.q_rows + self.place.z_plus(step) * self.z_rows
            self.put(self.acc.at[pl.ds(away, self.z_rows)], self.third.at[step - 1], self.place.along_z(step))

    def span(self):
        return self.p * self.p_rows + self.q * self.q_rows + self.place.z * self.z_rows

    def step_4(self):
        self.landed(3)
        total = self.acc[pl.ds(self.q * self.q_rows + self.place.z * self.z_rows, self.z_rows)].astype(full_type)
        for step in range(3):
            total += self.third[step].astype(full_type)
        mine = pl.ds(self.span(), self.z_rows)
        self.out[mine] = total.astype(low_type)
        for step in (1, 3, 2):
            self.put(self.out.at[mine], self.out.at[mine], self.place.along_z(step))

    def step_5(self):
        self.landed(3)
        mine = pl.ds(self.p * self.p_rows + self.q * self.q_rows, self.q_rows)
        self.put(self.out.at[mine], self.out.at[mine], self.q_next)

    def step_6(self):
        self.landed(1)
        mine = pl.ds(self.p * self.p_rows, self.p_rows)
        self.put(self.out.at[mine], self.out.at[mine], self.p_next)

    def finish(self):
        self.landed(1)
        for copy in self.copies:
            copy.wait_send()


class SmallGather:
    def __init__(self, place, all_ref, send, recv):
        self.place, self.all, self.send, self.recv = place, all_ref, send, recv
        self.line = (place.y * 2 + place.x) * 4
        self.copies = []

    def put(self, start, count, device):
        ref = self.all.at[pl.ds(start, count)]
        slot = len(self.copies)
        copy = remote(ref, ref, self.send.at[slot], self.recv.at[slot], device)
        copy.start()
        self.copies.append(copy)

    def step_1(self):
        for step in (1, 2, 3):
            self.put(self.line + self.place.z, 1, self.place.along_z(step))

    def step_2(self):
        for step in (1, 2, 3):
            ref = self.all.at[pl.ds(self.line + self.place.z_plus(step), 1)]
            remote(ref, ref, self.send.at[0], self.recv.at[3 - step], self.place.along_z(step)).wait_recv()
        self.put(self.line, 4, self.place.at(1 - self.place.x, self.place.y, self.place.z))

    def step_3(self):
        self.copies[3].wait_recv()
        self.put(self.place.y * 8, 8, self.place.at(self.place.x, 1 - self.place.y, self.place.z))

    def finish(self):
        self.copies[4].wait_recv()
        for copy in self.copies:
            copy.wait_send()


def transfer_kernel(
    factor_ref, grad_ref, small_ref,
    all_ref, sum_ref, small_all_ref,
    first, second, third, acc,
    g_send, g_recv, t_send, t_recv, r_send, r_recv, s_send, s_recv,
):
    place = Place()
    gathers = [Gather(place, all_ref, half, g_send, g_recv, t_send, t_recv) for half in range(2)]
    for half, gather in enumerate(gathers):
        own = gather.block(gather.q, gather.p, place.z)
        all_ref[place.head, half, own] = factor_ref[half]
    small = SmallGather(place, small_all_ref, s_send, s_recv)
    small_all_ref[small.line + place.z] = small_ref[...]
    reduces = [
        Reduce(
            place, slot, grad_ref.at[slot], sum_ref.at[slot], first.at[slot], second.at[slot], third.at[slot],
            acc.at[slot], r_send, r_recv,
        )
        for slot in range(4)
    ]
    meet(place)
    for gather in gathers:
        gather.start()
    for step in Z_ORDER[1:]:
        for gather in gathers:
            gather.z_step(step)
    for step in Z_ORDER:
        for gather in gathers:
            gather.p_step(step)
    small.step_1()
    reduces[0].step_1()
    reduces[1].step_1()
    for side in range(2):
        for step in Z_ORDER:
            for gather in gathers:
                gather.q_step(side, step)
    reduces[2].step_1()
    reduces[3].step_1()
    small.step_2()
    for name in ("step_2", "step_3", "step_4", "step_5", "step_6"):
        for pair in (0, 2):
            for reduce in reduces[pair : pair + 2]:
                getattr(reduce, name)()
        if name == "step_3":
            small.step_3()
    small.finish()
    for gather in gathers:
        for block in range(GROUP):
            gather.twin_landed(block)
    for reduce in reduces:
        reduce.finish()
    for gather in gathers:
        gather.finish()


def transfer(factor, grads, small):
    slots, rows, width = grads.shape
    vmem = pl.BlockSpec(memory_space=pltpu.VMEM)
    return pl.pallas_call(
        transfer_kernel,
        out_shape=(
            jax.ShapeDtypeStruct((2, 2, GROUP) + factor.shape[1:], low_type),
            jax.ShapeDtypeStruct(grads.shape, low_type),
            jax.ShapeDtypeStruct((GROUP,) + small.shape, full_type),
        ),
        in_specs=[vmem] * 3,
        out_specs=(vmem,) * 3,
        scratch_shapes=[
            pltpu.VMEM((slots, rows // 2, width), low_type),
            pltpu.VMEM((slots, rows // 4, width), low_type),
            pltpu.VMEM((slots, 3, rows // 16, width), low_type),
            pltpu.VMEM((slots, rows // 2, width), low_type),
            pltpu.SemaphoreType.DMA((2, 16)),
            pltpu.SemaphoreType.DMA((2, 16)),
            pltpu.SemaphoreType.DMA((2, 16)),
            pltpu.SemaphoreType.DMA((2, 16)),
            pltpu.SemaphoreType.DMA((slots, 10)),
            pltpu.SemaphoreType.DMA((slots, 10)),
            pltpu.SemaphoreType.DMA((5,)),
            pltpu.SemaphoreType.DMA((5,)),
        ],
        compiler_params=pltpu.CompilerParams(
            collective_id=0, has_side_effects=True, vmem_limit_bytes=48 * 2**20
        ),
    )(factor, grads, small)


def across_groups(values):
    size = lax.axis_size("dp")
    if size == GROUP:
        return values
    total = values
    moved = values
    for _ in range(size // GROUP - 1):
        moved = lax.ppermute(moved, "dp", [(i, (i + GROUP) % size) for i in range(size)])
        total = total + moved
    return total


def on_device(
    tokens,
    memory,
    query_weight,
    query_bias,
    key_weight,
    value_weight,
    value_bias,
    out_weight,
    out_bias,
    first_gain,
    first_shift,
    inner_weight,
    inner_bias,
    outer_weight,
    outer_bias,
    second_gain,
    second_shift,
    masked_rows,
    cotangent,
):
    seg_count, seq_len, feature_count = tokens.shape
    mem_len = memory.shape[1]
    all_rows = mem_len + seq_len
    masked = masked_rows.shape[1]
    local_heads = query_weight.shape[1] // HDIM
    score_scale = 1.0 / math.sqrt(HDIM)
    head = lax.axis_index("head")
    twin = lax.axis_size("head")

    def heads_view(values):
        return values.reshape(seg_count, values.shape[1], local_heads, HDIM)

    def flat_view(values):
        return values.reshape(seg_count, values.shape[1], local_heads * HDIM)

    def both(values):
        return lax.psum(values, "head")

    rows_low = jnp.concatenate([tokens, memory], axis=1)
    key_low = product("srd,de->sre", rows_low, key_weight).astype(low_type)
    value_low = (product("srd,de->sre", rows_low, value_weight) + value_bias).astype(low_type)
    key_heads = heads_view(key_low)
    value_heads = heads_view(value_low)

    pick = (masked_rows[:, :, None] == jnp.arange(seq_len, dtype=jnp.int32)).astype(low_type)
    rows_m = product("smt,std->smd", pick, tokens).astype(low_type)
    query_m = heads_view((product("smd,de->sme", rows_m, query_weight) + query_bias).astype(low_type))
    scores_m = product("smhd,skhd->shmk", query_m, key_heads) * score_scale
    probs_m = jax.nn.softmax(scores_m, axis=-1)
    probs_m_low = probs_m.astype(low_type)
    context_m = flat_view(product("shmk,skhd->smhd", probs_m_low, value_heads)).astype(low_type)
    attention_m = both(product("sme,ed->smd", context_m, out_weight)) + out_bias
    first_scaled, first_inverse = norm_stats(rows_m.astype(full_type) + attention_m)
    normed_m = first_scaled * first_gain + first_shift
    normed_m_low = normed_m.astype(low_type)
    inner_m = product("smd,df->smf", normed_m_low, inner_weight) + inner_bias
    active_m = jax.nn.gelu(inner_m, approximate=False).astype(low_type)
    outer_m = both(product("smf,fd->smd", active_m, outer_weight)) + outer_bias
    second_scaled, second_inverse = norm_stats(normed_m + outer_m)
    upstream = cotangent.astype(full_type)
    second_in_grad = norm_backward(upstream, second_scaled, second_inverse, second_gain.astype(full_type))
    outer_grad = second_in_grad.astype(low_type)
    inner_grad = (product("smd,fd->smf", outer_grad, outer_weight) * gelu_slope(inner_m)).astype(low_type)
    normed_grad = second_in_grad + both(product("smf,df->smd", inner_grad, inner_weight))
    first_in_grad = norm_backward(normed_grad, first_scaled, first_inverse, first_gain.astype(full_type))
    attention_grad = first_in_grad.astype(low_type)
    out_weight_grad = product("sme,smd->ed", context_m, attention_grad)
    context_grad = heads_view(product("smd,ed->sme", attention_grad, out_weight).astype(low_type))
    probs_grad = product("smhd,skhd->shmk", context_grad, value_heads)
    score_grad = (
        probs_m * (probs_grad - jnp.sum(probs_m * probs_grad, axis=-1, keepdims=True))
    ).astype(low_type)
    value_grad = flat_view(product("shmk,smhd->skhd", probs_m_low, context_grad)).astype(low_type)
    query_grad = flat_view(product("shmk,skhd->smhd", score_grad, key_heads) * score_scale).astype(low_type)
    key_grad = flat_view(product("shmk,smhd->skhd", score_grad, query_m) * score_scale).astype(low_type)
    query_weight_grad = product("smd,sme->de", rows_m, query_grad)
    key_weight_grad = product("srd,sre->de", rows_low, key_grad)
    value_weight_grad = product("srd,sre->de", rows_low, value_grad)

    small = jnp.stack(
        [
            row_sum(attention_grad.astype(full_type)),
            row_sum(normed_grad * first_scaled),
            row_sum(normed_grad),
            row_sum(upstream * second_scaled),
            row_sum(upstream),
            jnp.concatenate(
                [row_sum(query_grad.astype(full_type)), row_sum(value_grad.astype(full_type))]
            ),
            jnp.zeros((feature_count,), full_type),
            jnp.zeros((feature_count,), full_type),
        ]
    )

    input_part = product("sre,de->srd", key_grad, key_weight)
    input_part = input_part + product("sre,de->srd", value_grad, value_weight)
    masked_part = product("sme,de->smd", query_grad, query_weight) + jnp.where(head == 0, first_in_grad, 0.0)
    masked_high = masked_part.astype(low_type)
    masked_rest = (masked_part - masked_high.astype(full_type)).astype(low_type)
    spread = product("smt,smd->std", pick, masked_high) + product("smt,smd->std", pick, masked_rest)

    def exchange(values):
        return lax.psum_scatter(values.astype(low_type), "head", scatter_dimension=1, tiled=True)

    tokens_grad = exchange(input_part[:, :seq_len] + spread)
    memory_grad = exchange(input_part[:, seq_len:])

    query_heads = heads_view((product("srd,de->sre", rows_low, query_weight) + query_bias).astype(low_type))
    scores = product("sqhd,skhd->shqk", query_heads, key_heads) * score_scale
    raised = jnp.exp(scores - jnp.max(scores, axis=-1, keepdims=True))
    total = jnp.sum(raised, axis=-1, keepdims=True)
    context = product("shqk,skhd->shqd", raised.astype(low_type), value_heads) / total
    context = flat_view(jnp.swapaxes(context, 1, 2)).astype(low_type)
    attention_part = product("sre,ed->srd", context, out_weight)
    attention = jnp.concatenate(
        [exchange(attention_part[:, :seq_len]), exchange(attention_part[:, seq_len:])], axis=1
    ).astype(full_type)
    own_seq, own_mem = seq_len // twin, mem_len // twin
    rows_own = jnp.concatenate(
        [
            lax.dynamic_slice_in_dim(tokens, head * own_seq, own_seq, 1),
            lax.dynamic_slice_in_dim(memory, head * own_mem, own_mem, 1),
        ],
        axis=1,
    ).astype(full_type)
    scaled, _ = norm_stats(rows_own + attention + out_bias)
    normed = scaled * first_gain + first_shift
    normed_low = lax.all_gather(normed.astype(low_type), "head", axis=0, tiled=False)
    normed_low = jnp.concatenate(
        [normed_low[i, :, :own_seq] for i in range(twin)] + [normed_low[i, :, own_seq:] for i in range(twin)], axis=1
    )
    inner_act = product("srd,df->srf", normed_low, inner_weight) + inner_bias
    activated = jax.nn.gelu(inner_act, approximate=False).astype(low_type)
    outer_part = product("srf,fd->srd", activated, outer_weight)
    outer = jnp.concatenate(
        [exchange(outer_part[:, :seq_len]), exchange(outer_part[:, seq_len:])], axis=1
    ).astype(full_type)
    scaled, _ = norm_stats(normed + outer + outer_bias)
    result = (scaled * second_gain + second_shift).astype(low_type)
    layer_out, memory_out = result[:, :own_seq], result[:, own_seq:]

    factor = jnp.where(head == 0, normed_m_low, outer_grad)
    half = out_weight.shape[0]
    grads = jnp.stack(
        [
            jnp.concatenate([out_weight_grad[:, :half], out_weight_grad[:, half:]], axis=0),
            query_weight_grad,
            key_weight_grad,
            value_weight_grad,
        ]
    ).astype(low_type)
    factors, sums, smalls = transfer(factor, grads, small)
    normed_all = factors[0].reshape(-1, feature_count)
    outer_all = factors[1].reshape(-1, feature_count)
    inner_all = product("md,df->mf", normed_all, inner_weight) + inner_bias
    active_all = jax.nn.gelu(inner_all, approximate=False).astype(low_type)
    inner_grad_all = (product("md,fd->mf", outer_all, outer_weight) * gelu_slope(inner_all)).astype(low_type)
    outer_weight_grad = across_groups(product("mf,md->fd", active_all, outer_all))
    inner_weight_grad = across_groups(product("md,mf->df", normed_all, inner_grad_all))
    inner_bias_grad = across_groups(jnp.sum(inner_grad_all.astype(full_type), axis=0))
    outer_bias_grad = across_groups(jnp.sum(outer_all.astype(full_type), axis=0))
    sums = across_groups(sums.astype(full_type))
    smalls = across_groups(jnp.sum(smalls, axis=0))
    return (
        layer_out,
        memory_out,
        tokens_grad,
        memory_grad,
        sums[1],
        smalls[5, :half],
        sums[2],
        sums[3],
        smalls[5, half:],
        jnp.concatenate([sums[0, :half], sums[0, half:]], axis=1),
        smalls[0],
        smalls[1],
        smalls[2],
        inner_weight_grad,
        inner_bias_grad,
        outer_weight_grad,
        outer_bias_grad,
        smalls[3],
        smalls[4],
    )


def solution(mesh):
    return jax.shard_map(
        on_device,
        mesh=mesh,
        in_specs=(
            P("dp", None, None),
            P("dp", None, None),
            P(None, "head"),
            P("head"),
            P(None, "head"),
            P(None, "head"),
            P("head"),
            P("head", None),
            P(),
            P(),
            P(),
            P(None, "head"),
            P("head"),
            P("head", None),
            P(),
            P(),
            P(),
            P("dp", None),
            P("dp", None, None),
        ),
        out_specs=(
            P("dp", "head", None),
            P("dp", "head", None),
            P("dp", "head", None),
            P("dp", "head", None),
            P(None, "head"),
            P("head"),
            P(None, "head"),
            P(None, "head"),
            P("head"),
            P("head", None),
            P(),
            P(),
            P(),
            P(None, "head"),
            P("head"),
            P("head", None),
            P(),
            P(),
            P(),
        ),
        check_vma=False,
    )
```

time: 706 us -> 434 us (0.61)
  waiting for transfers between devices: 298 us -> 17.6 us
  blocking collectives: 146 us -> 5.25 us
  Pallas kernels: 0 us -> 106 us
  matrix products: 100 us -> 170 us
  other arithmetic: 81.9 us -> 46 us
  local copies, waits for them, and re-layouts: 56.9 us -> 65.9 us
    psum x1 -> x3, waiting for transfers between devices: 266 us -> 14.9 us  [both(): return lax.psum(values, 'head')]
    psum x2 -> x0, blocking collectives: 125 us -> none  [the longest x1 79.7 us: on_device(): lax.psum((query_weight_grad, query_bias_grad, key_weight_grad, value_weig...]
    pallas_call x0 -> x1, Pallas kernels: none -> 106 us  [transfer(): pl.pallas_call(transfer_kernel, out_shape=(jax.ShapeDtypeStruct((2, 2, GR...]
    dot_general x24 -> x33, matrix products: 100 us -> 167 us  [product(): return jnp.einsum(form, left, right, preferred_element_type=jnp.float32)]
    convert_element_type x15 -> x10, other arithmetic: 37.6 us -> 8.78 us  [the longest x1 4.17 us: on_device(): sums = across_groups(sums.astype(full_type))]
    all_gather x3 -> x1, waiting for transfers between devices: 26.3 us -> 1.8 us  [on_device(): lax.all_gather(normed.astype(low_type), 'head', axis=0, tiled=False)]
    scatter-add x1 -> x0, other arithmetic: 22.7 us -> none  [on_device(): token_upstream = jnp.zeros((seg_count, seq_len, feature_count), jnp.float...]
    unnamed x4 -> x1, blocking collectives: 15.3 us -> 5.25 us
  transfers between devices with their start and end apart: 8 -> 8, of which waited for: 5 -> 4; matrix products, arithmetic and copies ran while one was open for 10% -> 46% of each run, Pallas kernels for 0% -> 25%
where the time goes in v1:
time: 434 us; the launch traced here: 428 us
  matrix products  170 us (39%)
  Pallas kernels  106 us (24%)
  local copies, waits for them, and re-layouts  65.9 us (15%)
  other arithmetic  46 us (11%)
  waiting for transfers between devices  17.6 us (4%)
  between operations  16.2 us (4%)
  blocking collectives  5.25 us (1%)
    dot_general x33, matrix products, product(): return jnp.einsum(form, left, right, preferred_element_type=jnp.float32)  167 us
    pallas_call x1, Pallas kernels, transfer(): pl.pallas_call(transfer_kernel, out_shape=(jax.ShapeDtypeStruct((2, 2, GR...  106 us
    unnamed x168, local copies, waits for them, and re-layouts  16.9 us
    psum x3, waiting for transfers between devices, both(): return lax.psum(values, 'head')  14.9 us
    reduce_sum x1, other arithmetic, on_device(): total = jnp.sum(raised, axis=-1, keepdims=True)  9.16 us
  transfers between devices with their start and end apart: 8, of which 4 were waited for; matrix products, arithmetic and copies ran while one was open for 46% of the time, Pallas kernels for 25%

profile of v1, /device:TPU:0, one launch (start us, length us, event | category | flops | bytes accessed | tf_op | source)
XLA Modules:
  0.0 428.3 jit_solution(8657084805427651748)
XLA Ops:
  8.8 2.7 constant_dynamic-update-slice_fusion.1
  11.5 1.9 convolution_convert_fusion.3
  14.5 3.5 add_convert_fusion.2
  18.0 2.2 copy.86
  20.2 3.5 convolution_convert_fusion.2
  23.7 2.2 copy.85
  25.9 3.6 fusion.286
  29.5 2.7 convolution_convert_fusion.4
  33.6 3.5 add_convert_fusion.3
  37.8 2.2 copy.84
  40.0 10.5 %multiply_reduce_fusion = (f32[2,6,532]{2,1,0:T(8,128)}, f32[2,6,532,532]{2,3,1,0:T(8,128)}) fusion(bf16[2,532,6,64]{1,3,2,0:T(8,128)(2,1)} %bitcast.178, bf16[2,532,6,64]{1,3,2,0:T(8,128)(2,1)} %bitcast.173), kind=kOutput, calls=%fused_computation.29 | convolution fusion | flops 441511040 | bytes 15244992 | tf_op jit(solution)/shard_map/sqhd,skhd->shqk/dot_general | solution.py:43
  50.6 4.3 %all-reduce.9.cloned.1.call-done = f32[2,80,768]{2,1,0:T(8,128)} async-done(((f32[2,80,768]{2,1,0:T(8,128)}), f32[2,80,768]{2,1,0:T(8,128)}) %all-reduce.9.cloned.1.call-update) | async-done | bytes 491536 | tf_op jit(solution)/shard_map/psum | solution.py:417
  54.9 1.3 fusion.280
  58.7 3.4 fusion.39
  62.5 9.2 %fusion.17 = f32[2,6,532]{2,1,0:T(8,128)} fusion(f32[2,6,532,532]{2,3,1,0:T(8,128)} %get-tuple-element.141, f32[2,6,532]{2,1,0:T(8,128)} %get-tuple-element.140), kind=kLoop, calls=%fused_computation.30 | loop fusion | flops 10182480 | bytes 13636224 | tf_op jit(solution)/shard_map/reduce_sum | solution.py:491
  71.7 10.5 %all-reduce.11.cloned.1.call-done = f32[2,80,768]{2,1,0:T(8,128)} async-done(((f32[2,80,768]{2,1,0:T(8,128)}), f32[2,80,768]{2,1,0:T(8,128)}) %all-reduce.11.cloned.1.call-update) | async-done | bytes 491536 | tf_op jit(solution)/shard_map/psum | solution.py:417
  82.2 1.3 fusion.279
  84.6 2.0 broadcast_select_fusion
  86.7 4.5 %fusion.42 = f32[2,80,768]{2,1,0:T(8,128)} fusion(bf16[768,1536]{1,0:T(8,128)(2,1)S(1)} %copy-done, bf16[2,80,768]{2,1,0:T(8,128)(2,1)} %get-tuple-element.106, bf16[1536,768]{1,0:T(8,128)(2,1)} %param.32, f32[2,80,1536]{2,1,0:T(8,128)} %copy-done.77), kind=kOutput, calls=%fused_computation.73 | convolution fusion | flops 757432320 | bytes 6438912 | tf_op jit(solution)/shard_map/smf,df->smd/dot_general | solution.py:43
  91.2 9.6 %fusion.50 = bf16[2,532,6,64]{1,3,2,0:T(8,128)(2,1)} fusion(bf16[2,532,6,64]{1,3,2,0:T(8,128)(2,1)} %bitcast.189, f32[2,6,532,532]{2,3,1,0:T(8,128)} %get-tuple-element.141, f32[2,6,532]{2,1,0:T(8,128)} %get-tuple-element.140, f32[2,532,6]{1,2,0:T(8,128)} %bitcast.201), kind=kOutput, calls=%fused_computation.81 | convolution fusion | flops 445730880 | bytes 15270528 | tf_op jit(solution)/shard_map/shqk,skhd->shqd/dot_general | solution.py:43
  100.8 2.4 convolution_convert_fusion
  105.8 2.1 constant_dynamic-slice_fusion.4
  107.9 2.1 fusion.331
  110.0 1.5 slice.120
  112.8 1.5 copy.89
  114.3 5.3 %all-reduce = bf16[2,20,768]{2,0,1:T(2,128)(2,1)} all-reduce(bf16[2,20,768]{2,0,1:T(2,128)(2,1)} %copy.89), channel_id=3, replica_groups=mesh['dp'=16,'head'=2] {'head'}, use_global_device_ids=true, to_apply=%region_3.0.clone | all-reduce | flops 30720 | bytes 122880
  119.6 1.3 dynamic-slice
  122.3 1.6 fusion.285
  126.4 2.4 multiply_reduce_fusion.5
  130.5 2.1 convolution_convert_fusion.5
  133.7 1.7 copy.101
  135.4 3.9 convert_reduce_fusion.2
  141.2 1.8 convert_reduce_fusion.5
  143.0 1.4 multiply_convert_fusion.1
  147.7 3.9 fusion.73
  151.7 2.1 fusion.74
  157.3 3.0 pad_maximum_fusion.grad_ref
  161.1 1.7 copy-done.1
  162.7 106.3 %shard_map.330 = (bf16[2,2,16,80,768]{4,3,2,1,0:T(8,128)(2,1)}, bf16[4,768,384]{2,1,0:T(8,128)(2,1)S(1)}, f32[16,8,768]{2,1,0:T(8,128)S(1)}) custom-call(bf16[2,80,768]{2,1,0:T(8,128)(2,1)S(1)} %get-tuple-element.105.factor_ref, bf16[4,768,384]{2,1,0:T(8,128)(2,1)S(1)} %copy-done.1, f32[8,768]{1,0:T(8,128)S(1)} %stack.56.small_ref), custom_call_target="tpu_custom_call" | custom-call | tf_op jit(solution)/shard_map/pallas_call | solution.py:339
  269.0 4.4 %fusion.281 = (bf16[1,2,16,80,768]{4,3,2,1,0:T(8,128)(2,1)S(1)}, bf16[1,2,16,80,768]{4,3,2,1,0:T(8,128)(2,1)S(1)}) fusion(bf16[2,2,16,80,768]{4,3,2,1,0:T(8,128)(2,1)} %get-tuple-element.24), kind=kLoop, calls=%fused_computation.397 | loop fusion | bytes 15728640 | tf_op jit(solution)/shard_map/slice | solution.py:534
  273.5 6.5 %fusion.287 = f32[2560,1536]{1,0:T(8,128)S(1)} fusion(bf16[2560,768]{1,0:T(8,128)(2,1)S(1)} %bitcast.179, bf16[768,1536]{1,0:T(8,128)(2,1)S(1)} %copy-done), kind=kOutput, calls=%fused_computation.403 | convolution fusion | flops 6039797760 | bytes 22020096 | tf_op jit(solution)/shard_map/md,df->mf/dot_general | solution.py:43
  280.1 38.8 %fusion.23 = f32[1536,768]{1,0:T(8,128)} fusion(bf16[2560,768]{1,0:T(8,128)(2,1)S(1)} %bitcast.181, f32[2560,1536]{1,0:T(8,128)S(1)} %fusion.287, f32[1536]{0:T(1024)S(1)} %copy-done.67), kind=kOutput, calls=%fused_computation.37 | convolution fusion | flops 6299320320 | bytes 24385536 | tf_op jit(solution)/shard_map/mf,md->fd/dot_general | solution.py:43
  321.3 1.6 copy-done.4
  324.3 4.2 convert_element_type.275
  328.5 1.7 fusion.71
  330.3 1.9 multiply_reduce_fusion.4
  332.2 2.0 add_convert_fusion.1
  334.2 1.5 copy.92
  335.7 2.3 slice_bitcast_fusion.4
  338.1 1.5 convolution_add_fusion.2
  339.6 1.5 fusion.159
  341.1 3.3 convert_reduce_fusion.1
  344.4 1.9 fusion.36
  346.3 1.8 all-gather.2.cloned.1.call-done
  348.1 2.4 fusion.282
  351.6 4.2 fusion.64
  355.9 18.3 %fusion.51 = bf16[2,532,768]{2,1,0:T(8,128)(2,1)S(1)} fusion(bf16[1536,768]{1,0:T(8,128)(2,1)S(1)} %copy-done.76, f32[2,532,1536]{2,1,0:T(8,128)S(1)} %get-tuple-element.142, f32[1536]{0:T(1024)S(1)} %copy-done.68, u8[532,1536]{1,0:T(8,128)(4,1)S(1)} %get-tuple-element.83, u8[532,1536]{1,0:T(8,128)(4,1)S(1)} %get-tuple-element.82), kind=kOutput, calls=%fused_computation.86 | convolution fusion | flops 2627143680 | bytes 12171264 | tf_op jit(solution)/shard_map/srf,fd->srd/dot_general | solution.py:43
  377.3 2.7 slice.125
  380.1 16.6 %convert_reduce_fusion = (f32[1536]{0:T(1024)}, bf16[2560,1536]{1,0:T(8,128)(2,1)}) fusion(f32[2560,1536]{1,0:T(8,128)} %copy-done.78, f32[1536]{0:T(1024)S(1)} %copy-done.68, bf16[2560,768]{1,0:T(8,128)(2,1)} %bitcast.182, bf16[1536,768]{1,0:T(8,128)(2,1)} %param.32), kind=kOutput, calls=%fused_computation.26 | convolution fusion | flops 6090914304 | bytes 29896704 | tf_op jit(solution)/shard_map/md,fd->mf/dot_general | solution.py:43
  396.7 2.2 pad_maximum_fusion.1
  398.9 4.0 slice_bitcast_fusion
  402.9 10.4 %fusion.288 = f32[768,1536]{1,0:T(8,128)} fusion(bf16[2560,768]{1,0:T(8,128)(2,1)S(1)} %bitcast.180, bf16[2560,1536]{1,0:T(8,128)(2,1)} %get-tuple-element.144), kind=kOutput, calls=%fused_computation.404 | convolution fusion | flops 6039797760 | bytes 16515072 | tf_op jit(solution)/shard_map/md,mf->df/dot_general | solution.py:43
  414.1 1.4 constant_dynamic-slice_fusion
  415.5 2.4 fusion.277
  (246 shorter events, 40.1 us)
Async XLA Ops:
  7.2 49.8 %copy-start = (bf16[768,1536]{1,0:T(8,128)(2,1)S(1)}, bf16[768,1536]{1,0:T(8,128)(2,1)}, u32[]{:S(2)}) copy-start(bf16[768,1536]{1,0:T(8,128)(2,1)} %param.30) | copy-start | bytes 7077892
  7.2 6.6 %copy-start.43 = (bf16[2,20,768]{2,0,1:T(2,128)(2,1)S(1)}, bf16[2,20,768]{2,0,1:T(2,128)(2,1)}, u32[]{:S(2)}) copy-start(bf16[2,20,768]{2,0,1:T(2,128)(2,1)} %param.20) | copy-start | bytes 184324
  7.2 47.7 %all-reduce.9.cloned.1.call-start = ((), (), s32[]{:S(2)}) async-start(), calls=%async_computation.6 | async-start | bytes 983040 | tf_op jit(solution)/shard_map/psum | solution.py:417
  7.3 6.1 %copy-start.15 = (bf16[768,384]{1,0:T(8,128)(2,1)S(1)}, bf16[768,384]{1,0:T(8,128)(2,1)}, u32[]{:S(2)}) copy-start(bf16[768,384]{1,0:T(8,128)(2,1)} %param.21) | copy-start | bytes 1769476
  32.1 7.9 %copy-start.31 = (bf16[2,6,64,80]{3,2,1,0:T(8,128)(2,1)}, bf16[2,6,64,80]{3,2,1,0:T(8,128)(2,1)S(1)}, u32[]{:S(2)}) copy-start(bf16[2,6,64,80]{3,2,1,0:T(8,128)(2,1)S(1)} %convolution_convert_fusion.4) | copy-start | bytes 368644
  32.2 5.0 %copy-start.70 = (bf16[768]{0:T(1024)(128)(2,1)S(1)}, bf16[768]{0:T(1024)(128)(2,1)}, u32[]{:S(2)}) copy-start(bf16[768]{0:T(1024)(128)(2,1)} %param.28) | copy-start | bytes 4612
  32.2 5.0 %copy-start.71 = (bf16[768]{0:T(1024)(128)(2,1)S(1)}, bf16[768]{0:T(1024)(128)(2,1)}, u32[]{:S(2)}) copy-start(bf16[768]{0:T(1024)(128)(2,1)} %param.27) | copy-start | bytes 4612
  32.2 5.0 %copy-start.72 = (bf16[768]{0:T(1024)(128)(2,1)S(1)}, bf16[768]{0:T(1024)(128)(2,1)}, u32[]{:S(2)}) copy-start(bf16[768]{0:T(1024)(128)(2,1)} %param.29) | copy-start | bytes 4612
  32.2 5.0 %copy-start.73 = (bf16[768]{0:T(1024)(128)(2,1)S(1)}, bf16[768]{0:T(1024)(128)(2,1)}, u32[]{:S(2)}) copy-start(bf16[768]{0:T(1024)(128)(2,1)} %param.34) | copy-start | bytes 4612
  32.2 5.0 %copy-start.74 = (bf16[768]{0:T(1024)(128)(2,1)S(1)}, bf16[768]{0:T(1024)(128)(2,1)}, u32[]{:S(2)}) copy-start(bf16[768]{0:T(1024)(128)(2,1)} %param.33) | copy-start | bytes 4612
  32.2 5.6 %copy-start.69 = (bf16[1536]{0:T(1024)(128)(2,1)S(1)}, bf16[1536]{0:T(1024)(128)(2,1)}, u32[]{:S(2)}) copy-start(bf16[1536]{0:T(1024)(128)(2,1)} %param.31) | copy-start | bytes 9220
  33.4 48.8 %all-reduce.11.cloned.1.call-start = ((), (), s32[]{:S(2)}) async-start(), calls=%async_computation.7 | async-start | bytes 983040 | tf_op jit(solution)/shard_map/psum | solution.py:417
  37.1 17.7 %copy-start.36 = (f32[768]{0:T(1024)}, f32[768]{0:T(1024)S(1)}, u32[]{:S(2)}) copy-start(f32[768]{0:T(1024)S(1)} %convert_element_type.231) | copy-start | bytes 9220
  37.2 47.4 %copy-start.40 = (f32[768]{0:T(1024)}, f32[768]{0:T(1024)S(1)}, u32[]{:S(2)}) copy-start(f32[768]{0:T(1024)S(1)} %convert_element_type.233) | copy-start | bytes 9220
  37.2 89.2 %copy-start.38 = (f32[768]{0:T(1024)}, f32[768]{0:T(1024)S(1)}, u32[]{:S(2)}) copy-start(f32[768]{0:T(1024)S(1)} %convert_element_type.241) | copy-start | bytes 9220
  37.8 18.6 %copy-start.66 = (f32[1536]{0:T(1024)}, f32[1536]{0:T(1024)S(1)}, u32[]{:S(2)}) copy-start(f32[1536]{0:T(1024)S(1)} %convert_element_type.237) | copy-start | bytes 18436
  54.9 3.8 copy-start.75
  62.2 64.2 %all-reduce.13.cloned.1.call-start = ((), (), s32[]{:S(2)}) async-start(), calls=%async_computation.8 | async-start | bytes 983040 | tf_op jit(solution)/shard_map/psum | solution.py:417
  62.5 21.3 %copy-start.19 = (bf16[2,80,768]{2,1,0:T(8,128)(2,1)S(1)}, bf16[2,80,768]{2,1,0:T(8,128)(2,1)}, u32[]{:S(2)}) copy-start(bf16[2,80,768]{2,1,0:T(8,128)(2,1)} %param.37) | copy-start | bytes 737284
  91.1 237.4 %reduce-scatter.4.cloned.1.call-start = ((), (), s32[]{:S(2)}) async-start(), calls=%async_computation.3 | async-start | bytes 2359296 | tf_op jit(solution)/shard_map/reduce_scatter | solution.py:483
  104.4 22.0 %copy-start.47 = (f32[2,80]{1,0:T(2,128)S(1)}, f32[2,80]{1,0:T(2,128)}, u32[]{:S(2)}) copy-start(f32[2,80]{1,0:T(2,128)} %copy-done.46) | copy-start | bytes 1924
  105.7 242.4 %all-gather.2.cloned.1.call-start = ((), (), s32[]{:S(2)}) async-start(), calls=%async_computation.4 | async-start | bytes 2451456 | tf_op jit(solution)/shard_map/all_gather | solution.py:508
  126.4 6.1 %copy-start.32 = (bf16[2,6,64,80]{3,2,1,0:T(8,128)(2,1)S(1)}, bf16[2,6,64,80]{3,2,1,0:T(8,128)(2,1)}, u32[]{:S(2)}) copy-start(bf16[2,6,64,80]{3,2,1,0:T(8,128)(2,1)} %copy-done.31) | copy-start | bytes 368644
  128.9 6.5 %copy-start.61 = (f32[2,80]{1,0:T(2,128)}, f32[2,80]{1,0:T(2,128)S(1)}, u32[]{:S(2)}) copy-start(f32[2,80]{1,0:T(2,128)S(1)} %broadcast_multiply_fusion.2) | copy-start | bytes 1924
  135.4 3.9 copy-start.7
  135.4 3.9 copy-start.27
  135.4 3.9 copy-start.35
  135.4 3.9 copy-start.50
  141.2 4.3 %copy-start.57 = (f32[768]{0:T(1024)S(1)}, f32[768]{0:T(1024)}, u32[]{:S(2)}) copy-start(f32[768]{0:T(1024)} %get-tuple-element.103) | copy-start | bytes 9220
  141.2 4.9 %copy-start.17 = (bf16[384,768]{1,0:T(8,128)(2,1)S(1)}, bf16[384,768]{1,0:T(8,128)(2,1)}, u32[]{:S(2)}) copy-start(bf16[384,768]{1,0:T(8,128)(2,1)} %fusion.69) | copy-start | bytes 1769476
  147.7 3.9 copy-start.8
  147.7 3.9 copy-start.24
  151.7 4.0 copy-start.20
  156.1 4.1 copy-start.60
  269.0 4.5 %copy-start.2 = (bf16[4,768,384]{2,1,0:T(8,128)(2,1)}, bf16[4,768,384]{2,1,0:T(8,128)(2,1)S(1)}, u32[]{:S(2)}) copy-start(bf16[4,768,384]{2,1,0:T(8,128)(2,1)S(1)} %get-tuple-element.22) | copy-start | bytes 7077892
  273.5 6.5 %copy-start.12 = (bf16[1,2,16,80,768]{4,3,2,1,0:T(8,128)(2,1)}, bf16[1,2,16,80,768]{4,3,2,1,0:T(8,128)(2,1)S(1)}, u32[]{:S(2)}) copy-start(bf16[1,2,16,80,768]{4,3,2,1,0:T(8,128)(2,1)S(1)} %get-tuple-element.115) | copy-start | bytes 11796484
  273.5 6.5 %copy-start.14 = (bf16[1,2,16,80,768]{4,3,2,1,0:T(8,128)(2,1)}, bf16[1,2,16,80,768]{4,3,2,1,0:T(8,128)(2,1)S(1)}, u32[]{:S(2)}) copy-start(bf16[1,2,16,80,768]{4,3,2,1,0:T(8,128)(2,1)S(1)} %get-tuple-element.114) | copy-start | bytes 11796484
  273.5 6.5 %copy-start.67 = (f32[1536]{0:T(1024)S(1)}, f32[1536]{0:T(1024)}, u32[]{:S(2)}) copy-start(f32[1536]{0:T(1024)} %copy-done.66) | copy-start | bytes 18436
  280.0 38.8 %copy-start.78 = (f32[2560,1536]{1,0:T(8,128)}, f32[2560,1536]{1,0:T(8,128)S(1)}, u32[]{:S(2)}) copy-start(f32[2560,1536]{1,0:T(8,128)S(1)} %fusion.287) | copy-start | bytes 47185924
  280.0 38.8 %copy-start.9 = (bf16[2,6,64,532]{3,2,1,0:T(8,128)(2,1)S(1)}, bf16[2,6,64,532]{3,2,1,0:T(8,128)(2,1)}, u32[]{:S(2)}) copy-start(bf16[2,6,64,532]{3,2,1,0:T(8,128)(2,1)} %multiply_convert_fusion.1) | copy-start | bytes 2451460
  280.1 38.8 %copy-start.34 = (bf16[768,384]{1,0:T(8,128)(2,1)S(1)}, bf16[768,384]{1,0:T(8,128)(2,1)}, u32[]{:S(2)}) copy-start(bf16[768,384]{1,0:T(8,128)(2,1)} %param.23) | copy-start | bytes 1769476
  323.0 5.5 %copy-start.25 = (bf16[2,10,768]{2,1,0:T(8,128)(2,1)S(1)}, bf16[2,10,768]{2,1,0:T(8,128)(2,1)}, u32[]{:S(2)}) copy-start(bf16[2,10,768]{2,1,0:T(8,128)(2,1)} %get-tuple-element.147) | copy-start | bytes 92164
  323.0 5.5 %copy-start.29 = (bf16[2,10,768]{2,1,0:T(8,128)(2,1)S(1)}, bf16[2,10,768]{2,1,0:T(8,128)(2,1)}, u32[]{:S(2)}) copy-start(bf16[2,10,768]{2,1,0:T(8,128)(2,1)} %get-tuple-element.129) | copy-start | bytes 92164
  323.0 5.5 %copy-start.37 = (f32[768]{0:T(1024)S(1)}, f32[768]{0:T(1024)}, u32[]{:S(2)}) copy-start(f32[768]{0:T(1024)} %copy-done.36) | copy-start | bytes 9220
  324.3 7.8 %copy-start.41 = (f32[768]{0:T(1024)S(1)}, f32[768]{0:T(1024)}, u32[]{:S(2)}) copy-start(f32[768]{0:T(1024)} %copy-done.40) | copy-start | bytes 9220
  332.1 6.0 %copy-start.11 = (f32[2,80,768]{2,1,0:T(8,128)S(1)}, f32[2,80,768]{2,1,0:T(8,128)}, u32[]{:S(2)}) copy-start(f32[2,80,768]{2,1,0:T(8,128)} %copy-done.10) | copy-start | bytes 1474564
  332.1 6.0 %copy-start.21 = (bf16[2,6,64,80]{3,2,1,0:T(8,128)(2,1)S(1)}, bf16[2,6,64,80]{3,2,1,0:T(8,128)(2,1)}, u32[]{:S(2)}) copy-start(bf16[2,6,64,80]{3,2,1,0:T(8,128)(2,1)} %get-tuple-element.139) | copy-start | bytes 368644
  335.7 77.6 %all-reduce.15.cloned.1.call-start = ((), (), s32[]{:S(2)}) async-start(), calls=%async_computation.10 | async-start | bytes 245760
  339.5 4.9 %copy-start.5 = (f32[2,532,768]{2,1,0:T(8,128)S(1)}, f32[2,532,768]{2,1,0:T(8,128)}, u32[]{:S(2)}) copy-start(f32[2,532,768]{2,1,0:T(8,128)} %copy-done.4) | copy-start | bytes 9805828
  339.6 4.9 %copy-start.65 = (s32[2,80]{1,0:T(2,128)S(1)}, s32[2,80]{1,0:T(2,128)}, u32[]{:S(2)}) copy-start(s32[2,80]{1,0:T(2,128)} %param.36) | copy-start | bytes 1924
  346.3 5.3 %copy-start.68 = (f32[1536]{0:T(1024)S(1)}, f32[1536]{0:T(1024)}, u32[]{:S(2)}) copy-start(f32[1536]{0:T(1024)} %copy-done.66) | copy-start | bytes 18436
  351.6 4.2 copy-start.76
  355.8 20.2 %copy-start.42 = (f32[8,768]{1,0:T(8,128)S(1)}, f32[8,768]{1,0:T(8,128)}, u32[]{:S(2)}) copy-start(f32[8,768]{1,0:T(8,128)} %reduce_sum.253) | copy-start | bytes 73732
  376.0 39.4 %reduce-scatter.6.cloned.1.call-start = ((), (), s32[]{:S(2)}) async-start(), calls=%async_computation.5 | async-start | bytes 2359296 | tf_op jit(solution)/shard_map/reduce_scatter | solution.py:483
  380.0 16.7 %copy-start.18 = (f32[384,384]{1,0:T(8,128)S(1)}, f32[384,384]{1,0:T(8,128)}, u32[]{:S(2)}) copy-start(f32[384,384]{1,0:T(8,128)} %get-tuple-element.116) | copy-start | bytes 1769476
  380.0 41.0 %reduce-scatter.8.cloned.1.call-start = ((), (), s32[]{:S(2)}) async-start(), calls=%async_computation.9 | async-start | bytes 2359296 | tf_op jit(solution)/shard_map/reduce_scatter | solution.py:483
  398.9 4.0 copy-start.13
  402.9 12.6 %copy-start.26 = (bf16[2,10,768]{2,1,0:T(8,128)(2,1)S(1)}, bf16[2,10,768]{2,1,0:T(8,128)(2,1)}, u32[]{:S(2)}) copy-start(bf16[2,10,768]{2,1,0:T(8,128)(2,1)} %get-tuple-element.147) | copy-start | bytes 92164
  402.9 12.6 %copy-start.30 = (bf16[2,10,768]{2,1,0:T(8,128)(2,1)S(1)}, bf16[2,10,768]{2,1,0:T(8,128)(2,1)}, u32[]{:S(2)}) copy-start(bf16[2,10,768]{2,1,0:T(8,128)(2,1)} %get-tuple-element.129) | copy-start | bytes 92164
  402.9 12.6 %copy-start.45 = (f32[2,266]{1,0:T(2,128)S(1)}, f32[2,266]{1,0:T(2,128)}, u32[]{:S(2)}) copy-start(f32[2,266]{1,0:T(2,128)} %copy-done.44) | copy-start | bytes 6388
  402.9 12.6 %copy-start.48 = (f32[768]{0:T(1024)S(1)}, f32[768]{0:T(1024)}, u32[]{:S(2)}) copy-start(f32[768]{0:T(1024)} %convert_element_type.240) | copy-start | bytes 9220
  402.9 12.6 %copy-start.52 = (f32[2,266]{1,0:T(2,128)S(1)}, f32[2,266]{1,0:T(2,128)}, u32[]{:S(2)}) copy-start(f32[2,266]{1,0:T(2,128)} %copy-done.51) | copy-start | bytes 6388
  413.3 5.0 %copy-start.39 = (f32[768]{0:T(1024)S(1)}, f32[768]{0:T(1024)}, u32[]{:S(2)}) copy-start(f32[768]{0:T(1024)} %copy-done.38) | copy-start | bytes 9220
  413.3 5.0 %copy-start.58 = (f32[768]{0:T(1024)S(1)}, f32[768]{0:T(1024)}, u32[]{:S(2)}) copy-start(f32[768]{0:T(1024)} %convert_element_type.242) | copy-start | bytes 9220
  (23 other events, 42.8 us)
Sparse Core Ops, SparseCore 0:
  33.5 21.3 all-reduce.8
  62.3 19.8 all-reduce.10
  91.3 19.8 all-reduce.12
  113.2 10.2 reduce-scatter.3
  335.8 12.2 all-gather.1
  376.2 19.0 all-reduce.14
  397.6 10.2 reduce-scatter.5
  410.8 10.2 reduce-scatter.7
